TPU v7x, 128 devices: a whole 4x4x4 slice. The times are simulated.
128 devices in a mesh: row: 16 (over x, z), col: 8 (over y, core).
Axes of the slice: x: 4, y: 4, z: 4, core: 2. Of those that a mesh axis runs over, the one named last changes fastest.
Arguments:
- working: float32 [16384, 16384], P('row', 'col'), as said below
- step: int32 [1], replicated, may hold values from 0 to 122
Outputs:
- factored: float32 [16384, 16384], P('row', 'col')
Inputs may be any that keep to these rules, and one draw needn't show every extreme that they name: working is symmetric positive definite: a Matern covariance (smoothness 3/2) of sites on a grid, with scaled rows and a positive nugget on the diagonal.
All inputs are finite; a program needn't handle non-finite values.
Results may differ from a plain program's by a relative error of at most 0.0001.
Values sent between devices are 32-bit elements; how exact they have to be, the bound alone decides.
A program may use at most 128 MiB of HBM per device.

v0:
```python
import jax
import jax.numpy as jnp
from jax import lax
from jax.sharding import PartitionSpec as P

B = 128
STEPS = 6


def broadcast(block, axis, holder):
    block = jnp.where(lax.axis_index(axis) == holder, block, jnp.zeros_like(block))
    return lax.psum(block, axis)


def local(working, step):
    rows_count = lax.axis_size("row")
    cols_count = lax.axis_size("col")
    row_index = lax.axis_index("row")
    col_index = lax.axis_index("col")
    tile_rows = working.shape[0] // B
    tile_cols = working.shape[1] // B
    ratio = rows_count // cols_count
    row_of = jnp.repeat(jnp.arange(tile_rows, dtype=jnp.int32) * rows_count + row_index, B)
    col_of = jnp.repeat(jnp.arange(tile_cols, dtype=jnp.int32) * cols_count + col_index, B)
    lower_mask = row_of[:, None] >= col_of[None, :]
    start = step[0]
    column = lax.dynamic_slice_in_dim(working, start // cols_count * B, B, 1)
    for turn in range(STEPS):
        k = start + turn
        diag_local = lax.dynamic_slice_in_dim(column, k // rows_count * B, B, 0)
        diag = broadcast(diag_local, "row", k % rows_count)
        factor = jnp.linalg.cholesky(diag)
        solved = lax.linalg.triangular_solve(
            factor, column, left_side=False, lower=True, transpose_a=True
        )
        panel_mine = jnp.where((row_of > k)[:, None], solved, 0.0)
        panel_here = broadcast(panel_mine, "col", k % cols_count)
        slot = (row_index - col_index) // cols_count
        holds = row_index % cols_count == col_index
        selector = ((jnp.arange(ratio) == slot) & holds).astype(jnp.float32)
        buffer = panel_here.reshape(tile_rows, 1, B, B) * selector[None, :, None, None]
        panel_cols = lax.psum(buffer.reshape(tile_cols * B, B), "row")
        update = jnp.dot(panel_here, panel_cols.T, precision=lax.Precision.HIGHEST)
        working = working - jnp.where(lower_mask, update, 0.0)
        stacked = jnp.tile(factor, (tile_rows, 1))
        new_column = jnp.where(
            (row_of > k)[:, None], solved, jnp.where((row_of == k)[:, None], stacked, column)
        )
        slab = lax.dynamic_slice_in_dim(working, k // cols_count * B, B, 1)
        chosen = jnp.where(col_index == k % cols_count, new_column, slab)
        if turn + 1 < STEPS:
            following = k + 1
            where_next = following // cols_count * B
            working = lax.dynamic_update_slice_in_dim(working, chosen, k // cols_count * B, 1)
            column = lax.dynamic_slice_in_dim(working, where_next, B, 1)
        else:
            working = lax.dynamic_update_slice_in_dim(working, chosen, k // cols_count * B, 1)
    return working


def solution(mesh):
    placed = (P("row", "col"), P())
    return jax.shard_map(
        local, mesh=mesh, in_specs=placed, out_specs=P("row", "col"), check_vma=False
    )
```

profile of v0, /device:TPU:0, one launch (start us, length us, event | category | flops | bytes accessed | tf_op | source)
XLA Modules:
  0.0 1671.7 jit_solution(5050226096180740423)
XLA Ops:
  7.2 9.2 copy.8
  16.5 1.6 dynamic-slice_select_fusion.5
  18.3 83.4 %all-reduce.19.cloned.1.call-done = f32[128,128]{0,1:T(8,128)} async-done(((f32[128,128]{0,1:T(8,128)}), f32[128,128]{0,1:T(8,128)}) %all-reduce.19.cloned.1.call-update) | async-done | bytes 65552 | tf_op jit(solution)/shard_map/psum | solution.py:12
  103.5 11.7 cholesky.104
  116.7 9.8 custom-call.10
  126.5 2.5 select_select_fusion.5
  129.1 60.0 %all-reduce.21.cloned.1.call-done = f32[1024,128]{0,1:T(8,128)} async-done(((f32[1024,128]{0,1:T(8,128)}), f32[1024,128]{0,1:T(8,128)}) %all-reduce.21.cloned.1.call-update) | async-done | bytes 524304 | tf_op jit(solution)/shard_map/psum | solution.py:12
  189.1 1.2 copy.37
  190.4 1.4 bitcast_multiply_fusion.5
  192.5 86.2 %all-reduce.23.cloned.1.call-done = f32[2048,128]{1,0:T(8,128)} async-done(((f32[2048,128]{1,0:T(8,128)}), f32[2048,128]{1,0:T(8,128)}) %all-reduce.23.cloned.1.call-update) | async-done | bytes 1048592 | tf_op jit(solution)/shard_map/psum | solution.py:42
  278.7 9.9 fusion
  288.7 1.3 fusion.23
  290.0 3.4 copy-done
  294.2 80.1 %all-reduce.25.cloned.1.call-done = f32[128,128]{0,1:T(8,128)} async-done(((f32[128,128]{0,1:T(8,128)}), f32[128,128]{0,1:T(8,128)}) %all-reduce.25.cloned.1.call-update) | async-done | bytes 65552 | tf_op jit(solution)/shard_map/psum | solution.py:12
  376.2 11.7 cholesky.115
  389.3 9.8 custom-call.11
  399.2 2.5 select_select_fusion.4
  401.7 60.1 %all-reduce.27.cloned.1.call-done = f32[1024,128]{0,1:T(8,128)} async-done(((f32[1024,128]{0,1:T(8,128)}), f32[1024,128]{0,1:T(8,128)}) %all-reduce.27.cloned.1.call-update) | async-done | bytes 524304 | tf_op jit(solution)/shard_map/psum | solution.py:12
  463.0 1.4 bitcast_multiply_fusion.4
  465.2 86.1 %all-reduce.29.cloned.1.call-done = f32[2048,128]{1,0:T(8,128)} async-done(((f32[2048,128]{1,0:T(8,128)}), f32[2048,128]{1,0:T(8,128)}) %all-reduce.29.cloned.1.call-update) | async-done | bytes 1048592 | tf_op jit(solution)/shard_map/psum | solution.py:42
  551.2 9.9 fusion.1
  561.2 1.3 fusion.20
  562.6 3.4 copy-done.1
  566.7 80.2 %all-reduce.31.cloned.1.call-done = f32[128,128]{0,1:T(8,128)} async-done(((f32[128,128]{0,1:T(8,128)}), f32[128,128]{0,1:T(8,128)}) %all-reduce.31.cloned.1.call-update) | async-done | bytes 65552 | tf_op jit(solution)/shard_map/psum | solution.py:12
  648.7 11.7 cholesky.126
  661.9 9.8 custom-call.12
  671.7 2.5 select_select_fusion.3
  674.2 60.1 %all-reduce.33.cloned.1.call-done = f32[1024,128]{0,1:T(8,128)} async-done(((f32[1024,128]{0,1:T(8,128)}), f32[1024,128]{0,1:T(8,128)}) %all-reduce.33.cloned.1.call-update) | async-done | bytes 524304 | tf_op jit(solution)/shard_map/psum | solution.py:12
  734.3 1.2 copy.39
  735.6 1.4 bitcast_multiply_fusion.3
  737.4 86.6 %all-reduce.35.cloned.1.call-done = f32[2048,128]{1,0:T(8,128)} async-done(((f32[2048,128]{1,0:T(8,128)}), f32[2048,128]{1,0:T(8,128)}) %all-reduce.35.cloned.1.call-update) | async-done | bytes 1048592 | tf_op jit(solution)/shard_map/psum | solution.py:42
  823.9 9.9 fusion.2
  833.9 1.3 fusion.17
  835.3 3.4 copy-done.2
  839.5 80.2 %all-reduce.37.cloned.1.call-done = f32[128,128]{0,1:T(8,128)} async-done(((f32[128,128]{0,1:T(8,128)}), f32[128,128]{0,1:T(8,128)}) %all-reduce.37.cloned.1.call-update) | async-done | bytes 65552 | tf_op jit(solution)/shard_map/psum | solution.py:12
  921.4 11.7 cholesky.137
  934.6 9.8 custom-call.13
  944.4 2.5 select_select_fusion.2
  947.0 60.1 %all-reduce.39.cloned.1.call-done = f32[1024,128]{0,1:T(8,128)} async-done(((f32[1024,128]{0,1:T(8,128)}), f32[1024,128]{0,1:T(8,128)}) %all-reduce.39.cloned.1.call-update) | async-done | bytes 524304 | tf_op jit(solution)/shard_map/psum | solution.py:12
  1008.3 1.4 bitcast_multiply_fusion.2
  1010.2 86.4 %all-reduce.41.cloned.1.call-done = f32[2048,128]{1,0:T(8,128)} async-done(((f32[2048,128]{1,0:T(8,128)}), f32[2048,128]{1,0:T(8,128)}) %all-reduce.41.cloned.1.call-update) | async-done | bytes 1048592 | tf_op jit(solution)/shard_map/psum | solution.py:42
  1096.5 9.9 fusion.3
  1106.5 1.3 fusion.14
  1107.9 3.4 copy-done.3
  1112.1 80.2 %all-reduce.43.cloned.1.call-done = f32[128,128]{0,1:T(8,128)} async-done(((f32[128,128]{0,1:T(8,128)}), f32[128,128]{0,1:T(8,128)}) %all-reduce.43.cloned.1.call-update) | async-done | bytes 65552 | tf_op jit(solution)/shard_map/psum | solution.py:12
  1194.0 11.7 cholesky.148
  1207.2 9.8 custom-call.14
  1217.0 2.5 select_select_fusion.1
  1219.6 60.1 %all-reduce.45.cloned.1.call-done = f32[1024,128]{0,1:T(8,128)} async-done(((f32[1024,128]{0,1:T(8,128)}), f32[1024,128]{0,1:T(8,128)}) %all-reduce.45.cloned.1.call-update) | async-done | bytes 524304 | tf_op jit(solution)/shard_map/psum | solution.py:12
  1280.9 1.4 bitcast_multiply_fusion.1
  1282.9 86.2 %all-reduce.47.cloned.1.call-done = f32[2048,128]{1,0:T(8,128)} async-done(((f32[2048,128]{1,0:T(8,128)}), f32[2048,128]{1,0:T(8,128)}) %all-reduce.47.cloned.1.call-update) | async-done | bytes 1048592 | tf_op jit(solution)/shard_map/psum | solution.py:42
  1369.1 9.9 fusion.4
  1379.1 1.3 fusion.11
  1380.5 3.4 copy-done.4
  1384.6 80.2 %all-reduce.49.cloned.1.call-done = f32[128,128]{0,1:T(8,128)} async-done(((f32[128,128]{0,1:T(8,128)}), f32[128,128]{0,1:T(8,128)}) %all-reduce.49.cloned.1.call-update) | async-done | bytes 65552 | tf_op jit(solution)/shard_map/psum | solution.py:12
  1466.6 11.7 cholesky.159
  1479.8 9.8 custom-call.15
  1489.6 2.5 select_select_fusion
  1492.3 59.9 %all-reduce.51.cloned.1.call-done = f32[1024,128]{0,1:T(8,128)} async-done(((f32[1024,128]{0,1:T(8,128)}), f32[1024,128]{0,1:T(8,128)}) %all-reduce.51.cloned.1.call-update) | async-done | bytes 524304 | tf_op jit(solution)/shard_map/psum | solution.py:12
  1553.5 1.3 bitcast_multiply_fusion
  1554.9 86.8 %all-reduce.53.cloned.1.call-done = f32[2048,128]{1,0:T(8,128)} async-done(((f32[2048,128]{1,0:T(8,128)}), f32[2048,128]{1,0:T(8,128)}) %all-reduce.53.cloned.1.call-update) | async-done | bytes 1048592 | tf_op jit(solution)/shard_map/psum | solution.py:42
  1641.7 11.6 fusion.5
  1653.3 2.2 fusion.8
  1655.6 9.1 copy.30
  (99 shorter events, 31.8 us)
Async XLA Ops:
  6.5 95.2 %all-reduce.19.cloned.1.call-start = ((), (), s32[]{:S(2)}) async-start(), calls=%async_computation | async-start | bytes 131072 | tf_op jit(solution)/shard_map/psum | solution.py:12
  18.1 171.0 %all-reduce.21.cloned.1.call-start = ((), (), s32[]{:S(2)}) async-start(), calls=%async_computation.1 | async-start | bytes 1048576 | tf_op jit(solution)/shard_map/psum | solution.py:12
  129.0 149.7 %all-reduce.23.cloned.1.call-start = ((), (), s32[]{:S(2)}) async-start(), calls=%async_computation.2 | async-start | bytes 2097152 | tf_op jit(solution)/shard_map/psum | solution.py:42
  191.8 182.6 %all-reduce.25.cloned.1.call-start = ((), (), s32[]{:S(2)}) async-start(), calls=%async_computation.3 | async-start | bytes 131072 | tf_op jit(solution)/shard_map/psum | solution.py:12
  290.0 3.4 copy-start
  294.2 167.6 %all-reduce.27.cloned.1.call-start = ((), (), s32[]{:S(2)}) async-start(), calls=%async_computation.4 | async-start | bytes 1048576 | tf_op jit(solution)/shard_map/psum | solution.py:12
  401.6 149.6 %all-reduce.29.cloned.1.call-start = ((), (), s32[]{:S(2)}) async-start(), calls=%async_computation.5 | async-start | bytes 2097152 | tf_op jit(solution)/shard_map/psum | solution.py:42
  464.4 182.5 %all-reduce.31.cloned.1.call-start = ((), (), s32[]{:S(2)}) async-start(), calls=%async_computation.6 | async-start | bytes 131072 | tf_op jit(solution)/shard_map/psum | solution.py:12
  562.5 3.4 copy-start.1
  566.7 167.7 %all-reduce.33.cloned.1.call-start = ((), (), s32[]{:S(2)}) async-start(), calls=%async_computation.7 | async-start | bytes 1048576 | tf_op jit(solution)/shard_map/psum | solution.py:12
  674.2 149.7 %all-reduce.35.cloned.1.call-start = ((), (), s32[]{:S(2)}) async-start(), calls=%async_computation.8 | async-start | bytes 2097152 | tf_op jit(solution)/shard_map/psum | solution.py:42
  737.0 182.7 %all-reduce.37.cloned.1.call-start = ((), (), s32[]{:S(2)}) async-start(), calls=%async_computation.9 | async-start | bytes 131072 | tf_op jit(solution)/shard_map/psum | solution.py:12
  835.3 3.4 copy-start.2
  839.4 167.7 %all-reduce.39.cloned.1.call-start = ((), (), s32[]{:S(2)}) async-start(), calls=%async_computation.10 | async-start | bytes 1048576 | tf_op jit(solution)/shard_map/psum | solution.py:12
  946.9 149.6 %all-reduce.41.cloned.1.call-start = ((), (), s32[]{:S(2)}) async-start(), calls=%async_computation.11 | async-start | bytes 2097152 | tf_op jit(solution)/shard_map/psum | solution.py:42
  1009.7 182.5 %all-reduce.43.cloned.1.call-start = ((), (), s32[]{:S(2)}) async-start(), calls=%async_computation.12 | async-start | bytes 131072 | tf_op jit(solution)/shard_map/psum | solution.py:12
  1107.9 3.4 copy-start.3
  1112.0 167.7 %all-reduce.45.cloned.1.call-start = ((), (), s32[]{:S(2)}) async-start(), calls=%async_computation.13 | async-start | bytes 1048576 | tf_op jit(solution)/shard_map/psum | solution.py:12
  1219.5 149.6 %all-reduce.47.cloned.1.call-start = ((), (), s32[]{:S(2)}) async-start(), calls=%async_computation.14 | async-start | bytes 2097152 | tf_op jit(solution)/shard_map/psum | solution.py:42
  1282.3 182.5 %all-reduce.49.cloned.1.call-start = ((), (), s32[]{:S(2)}) async-start(), calls=%async_computation.15 | async-start | bytes 131072 | tf_op jit(solution)/shard_map/psum | solution.py:12
  1380.4 3.4 copy-start.4
  1384.6 167.7 %all-reduce.51.cloned.1.call-start = ((), (), s32[]{:S(2)}) async-start(), calls=%async_computation.16 | async-start | bytes 1048576 | tf_op jit(solution)/shard_map/psum | solution.py:12
  1492.1 149.6 %all-reduce.53.cloned.1.call-start = ((), (), s32[]{:S(2)}) async-start(), calls=%async_computation.17 | async-start | bytes 2097152 | tf_op jit(solution)/shard_map/psum | solution.py:42
Sparse Core Ops, SparseCore 0:
  18.3 83.3 all-reduce.18
  129.1 59.9 all-reduce.20
  192.4 86.2 all-reduce.22
  294.3 80.0 all-reduce.24
  401.8 59.9 all-reduce.26
  464.9 86.2 all-reduce.28
  566.8 80.0 all-reduce.30
  674.3 59.9 all-reduce.32
  737.6 86.2 all-reduce.34
  839.5 80.0 all-reduce.36
  947.0 60.0 all-reduce.38
  1010.2 86.2 all-reduce.40
  1112.1 80.0 all-reduce.42
  1219.6 59.9 all-reduce.44
  1282.8 86.3 all-reduce.46
  1384.7 80.0 all-reduce.48
  1492.2 59.9 all-reduce.50
  1555.3 86.2 all-reduce.52
where the time goes:
time: 1680 us; the launch traced here: 1670 us
  waiting for transfers between devices  1360 us (81%)
  other arithmetic  165 us (10%)
  matrix products  76.1 us (5%)
  local copies, waits for them, and re-layouts  49.2 us (3%)
    psum x12, waiting for transfers between devices, broadcast(): return lax.psum(block, axis)  845 us
    psum x6, waiting for transfers between devices, local(): panel_cols = lax.psum(buffer.reshape(tile_cols * B, B), 'row')  518 us
    another operation x18, other arithmetic, local(): factor = jnp.linalg.cholesky(diag)  74.8 us
    another operation x12, other arithmetic, local(): lax.linalg.triangular_solve(factor, column, left_side=False, lower=True,...  63.1 us
    dot_general x6, matrix products, local(): update = jnp.dot(panel_here, panel_cols.T, precision=lax.Precision.HIGHEST)  61.3 us
  transfers between devices with their start and end apart: 18, of which 18 were waited for; matrix products, arithmetic and copies ran while one was open for 0% of the time, Pallas kernels for 0%

commit v1 on v0

v1 whole, which is shorter than its diff:
```python
import functools

import jax
import jax.numpy as jnp
from jax import lax
from jax.experimental import pallas as pl
from jax.experimental.pallas import tpu as pltpu
from jax.sharding import PartitionSpec as P

B = 128
STEPS = 6
W = B * STEPS
F32 = jnp.float32
BF16 = jnp.bfloat16
MESH = pl.DeviceIdType.MESH
HIGHEST = lax.Precision.HIGHEST
NT = (((1,), (1,)), ((), ()))
NN = (((1,), (0,)), ((), ()))


def factor_tile(tile):
    chunk = 8
    rest = tile
    other = (
        lax.broadcasted_iota(jnp.int32, (B, B), 0) == lax.broadcasted_iota(jnp.int32, (B, B), 1)
    ).astype(F32)
    uppers, inverses = [], []
    for first in range(0, B, chunk):
        rows = B - first
        row = lax.broadcasted_iota(jnp.int32, (rows, B), 0)
        coefs = [
            jnp.broadcast_to(rest[:, first + i : first + i + 1], (rows, B)) for i in range(chunk)
        ]
        scales = []
        for j in range(chunk):
            scale = lax.rsqrt(coefs[j][j : j + 1, :])
            scales.append(scale)
            factor = jnp.where(row > j, coefs[j] * (scale * scale), 0.0)
            rest = rest - factor * rest[j : j + 1, :]
            other = other - factor * other[j : j + 1, :]
            for i in range(j + 1, chunk):
                coefs[i] = coefs[i] - factor * coefs[i][j : j + 1, :]
        scale = jnp.concatenate(scales, 0)
        sub = lax.broadcasted_iota(jnp.int32, (chunk, B), 0)
        lane = lax.broadcasted_iota(jnp.int32, (chunk, B), 1)
        uppers.append(jnp.where(lane >= first + sub, rest[:chunk] * scale, 0.0))
        inverses.append(other[:chunk] * scale)
        rest, other = rest[chunk:], other[chunk:]
    return jnp.concatenate(uppers, 0), jnp.concatenate(inverses, 0)


class Ring:
    MESSAGES = (
        (
            ((0, 0), None, (1, 0)),
            ((0, 0), None, (-1, 0)),
            ((0, 0), None, (0, 1)),
            ((0, 0), None, (0, -1)),
        ),
        (
            ((-1, 0), 0, (1, 0)),
            ((1, 0), 1, (-1, 0)),
            ((0, -1), 0, (0, 1)),
            ((0, 1), 1, (0, -1)),
            ((-1, 0), None, (0, 1)),
            ((-1, 0), None, (0, -1)),
            ((1, 0), None, (0, 1)),
            ((1, 0), None, (0, -1)),
        ),
        (
            ((2, 0), None, (0, 1)),
            ((2, 0), None, (0, -1)),
            ((-1, -1), 0, (0, 1)),
            ((1, -1), 0, (0, 1)),
            ((-1, 1), 1, (0, -1)),
            ((1, 1), 1, (0, -1)),
        ),
        (
            ((2, -1), 0, (0, 1)),
            ((2, 1), 1, (0, -1)),
        ),
    )
    COUNT = 20

    def __init__(self, row, col, view, own, send_sem, recv_sem):
        core = lax.rem(col, 2)
        x, z = row // 4, lax.rem(row, 4)
        self.u = z + core * (x - z)
        self.v = x + core * (z - x)
        self.su, self.sv = 1 + 3 * core, 4 - 3 * core
        self.col, self.view, self.own = col, view, own
        self.send_sem, self.recv_sem = send_sem, recv_sem

    def index(self, du, dv):
        return self.su * lax.rem(self.u + du + 4, 4) + self.sv * lax.rem(self.v + dv + 4, 4)

    def copy(self, number, message, receiving):
        (du, dv), part, (au, av) = message
        if receiving:
            du, dv = du - au, dv - av
        block = self.index(du, dv)
        dst = self.view(block, part)
        src = self.own if (du, dv) == (0, 0) and not receiving and self.own is not None else dst
        return pltpu.make_async_remote_copy(
            src_ref=src,
            dst_ref=dst,
            send_sem=self.send_sem.at[number],
            recv_sem=self.recv_sem.at[number],
            device_id=(self.index(au, av), self.col),
            device_id_type=MESH,
        )

    def numbered(self, tick):
        base = sum(len(m) for m in self.MESSAGES[:tick])
        return [(base + i, m) for i, m in enumerate(self.MESSAGES[tick])]

    def tick(self, tick):
        if tick > 0:
            for number, message in self.numbered(tick - 1):
                self.copy(number, message, True).wait_recv()
        if tick < len(self.MESSAGES):
            for number, message in self.numbered(tick):
                self.copy(number, message, False).start()

    def finish(self):
        for tick in range(len(self.MESSAGES)):
            for number, message in self.numbered(tick):
                self.copy(number, message, False).wait_send()


def gather_kernel(
    idx, tile, strip, slab,
    upper_o, inverse_o, lower_o, rout, cout,
    dbuf, dcol, dcg, whole, rbuf, bst,
    d1s, d1r, a1s, a1r, d2s, d2r, d3s, d3r, sibs, sibr, rs, rr, cs, cr, local,
):
    p, q = lax.axis_index("row"), lax.axis_index("col")
    core, y = lax.rem(q, 2), q // 2
    sibling = q + 1 - 2 * core

    barrier = pltpu.get_barrier_semaphore()
    for d in range(1, 16):
        pl.semaphore_signal(barrier, inc=1, device_id=(lax.rem(p + d, 16), q), device_id_type=MESH)
    for d in range(1, 8):
        pl.semaphore_signal(barrier, inc=1, device_id=(p, lax.rem(q + d, 8)), device_id_type=MESH)
    pl.semaphore_wait(barrier, 22)

    def remote(src, dst, send, recv, device):
        return pltpu.make_async_remote_copy(
            src_ref=src, dst_ref=dst, send_sem=send, recv_sem=recv,
            device_id=device, device_id_type=MESH,
        )

    def diag(d, slot):
        to = lax.rem(p + d, 16)
        rows = pl.ds(pl.multiple_of(8 * to, 8), 8)
        return remote(tile.at[rows, :], dbuf.at[slot], d1s.at[d], d1r.at[d], (to, q))

    def piece(d, slot):
        to = lax.rem(p + d, 16)
        columns = pl.ds(pl.multiple_of(B * to, B), B)
        return remote(strip.at[:, columns], rbuf.at[slot], a1s.at[d], a1r.at[d], (to, q))

    def spread(d, slot):
        to = lax.rem(q + d, 8)
        return remote(dcol, dcg.at[slot], d2s.at[d], d2r.at[d], (p, to))

    for d in range(1, 16):
        diag(d, p).start()
    for d in range(1, 16):
        piece(d, p).start()
    own_piece = pltpu.make_async_copy(
        strip.at[:, pl.ds(pl.multiple_of(B * p, B), B)], rbuf.at[p], local.at[0]
    )
    own_piece.start()
    own_slab = pltpu.make_async_copy(slab, cout.at[q], local.at[1])
    own_slab.start()
    dbuf[p] = tile[pl.ds(pl.multiple_of(8 * p, 8), 8), :]
    for d in range(1, 16):
        diag(d, lax.rem(p + 16 - d, 16)).wait_recv()
    for s in range(STEPS):
        block = dbuf[idx[s]]
        dcol[s] = block
        dcg[q, s] = block
    for d in range(1, 8):
        spread(d, q).start()

    def slot(dy):
        return lax.rem(y + dy + 4, 4) * 2 + core

    def part_of(block, part):
        return cout.at[block] if part is None else cout.at[block, pl.ds(512 * part, 512), :]

    def along(n, dy, part, ay, receiving):
        block = slot(dy - ay if receiving else dy)
        dst = part_of(block, part)
        src = slab if dy == 0 and not receiving else dst
        return remote(src, dst, cs.at[n], cr.at[n], (p, slot(ay)))

    def across(n, dy, receiving):
        block = slot(dy) + 1 - 2 * core if receiving else slot(dy)
        src = slab if dy == 0 and not receiving else cout.at[block]
        return remote(src, cout.at[block], cs.at[n], cr.at[n], (p, sibling))

    along_messages = ((0, 0, None, 1), (1, 0, None, -1), (3, -1, 0, 1), (4, 1, 1, -1))
    across_messages = ((2, 0), (5, -1), (6, 1), (7, 2))

    def columns_tick(tick):
        if tick == 0:
            along(*along_messages[0], False).start()
            along(*along_messages[1], False).start()
            across(*across_messages[0], False).start()
        elif tick == 1:
            along(*along_messages[0], True).wait_recv()
            along(*along_messages[1], True).wait_recv()
            along(*along_messages[2], False).start()
            along(*along_messages[3], False).start()
            across(*across_messages[1], False).start()
            across(*across_messages[2], False).start()
        elif tick == 2:
            along(*along_messages[2], True).wait_recv()
            along(*along_messages[3], True).wait_recv()
            across(*across_messages[3], False).start()
        else:
            for message in across_messages:
                across(*message, True).wait_recv()
            for message in along_messages:
                along(*message, False).wait_send()
            for message in across_messages:
                across(*message, False).wait_send()

    for d in range(1, 8):
        spread(d, lax.rem(q + 8 - d, 8)).wait_recv()
    half = pl.ds(3 * core, 3)
    for b in range(STEPS):
        whole[half, p, :, b * B : (b + 1) * B] = dcg[idx[STEPS + b], half]

    def diag_view(block, part):
        if part is None:
            return whole.at[half, block]
        return whole.at[half, block, :, pl.ds(384 * part, 384)]

    def row_view(block, part):
        return rout.at[block] if part is None else rout.at[block, pl.ds(384 * part, 384), :]

    diag_ring = Ring(p, q, diag_view, None, d3s, d3r)
    row_ring = Ring(p, q, row_view, bst, rs, rr)
    diag_ring.tick(0)
    columns_tick(0)

    own_piece.wait()
    for d in range(1, 16):
        piece(d, lax.rem(p + 16 - d, 16)).wait_recv()
    for s in range(STEPS):
        bst[s * B : (s + 1) * B, :] = rbuf[idx[s]]
    own_rows = pltpu.make_async_copy(bst, rout.at[p], local.at[2])
    own_rows.start()
    diag_ring.tick(1)
    diag_ring.tick(2)
    diag_ring.tick(3)
    row_ring.tick(0)
    diag_ring.tick(4)
    other = pl.ds(3 - 3 * core, 3)
    to_sibling = remote(whole.at[half], whole.at[half], sibs, sibr, (p, sibling))
    from_sibling = remote(whole.at[other], whole.at[other], sibs, sibr, (p, sibling))
    to_sibling.start()
    columns_tick(1)
    from_sibling.wait_recv()
    to_sibling.wait_send()
    diag_ring.finish()

    def step(k, carry):
        here = pl.ds(pl.multiple_of(k * B, B), B)
        upper, inverse = factor_tile(whole[k, :, :, here].reshape(B, B))
        upper_o[k] = upper
        inverse_o[k] = inverse
        for i in range(STEPS):

            @pl.when(k == i)
            def _():
                if i < STEPS - 1:
                    left = STEPS - 1 - i
                    below = whole[i + 1 :, :, :, i * B : (i + 1) * B].reshape(left * B, B)
                    solved = lax.dot_general(
                        below, inverse_o[i], NT, precision=HIGHEST, preferred_element_type=F32
                    )
                    lower_o[i, (i + 1) * B :, :] = solved
                    update = lax.dot_general(
                        solved, solved, NT, precision=HIGHEST, preferred_element_type=F32
                    )
                    whole[i + 1 :, :, :, (i + 1) * B :] = whole[
                        i + 1 :, :, :, (i + 1) * B :
                    ] - update.reshape(left, 16, 8, left * B)
                if i == 0:
                    row_ring.tick(1)
                    columns_tick(2)
                if i == 2:
                    row_ring.tick(2)
                if i == 4:
                    row_ring.tick(3)
                if i == 5:
                    row_ring.tick(4)

        return carry

    lax.fori_loop(0, STEPS, step, 0)
    columns_tick(3)
    row_ring.finish()
    for d in range(1, 16):
        diag(d, p).wait_send()
        piece(d, p).wait_send()
    for d in range(1, 8):
        spread(d, q).wait_send()
    own_slab.wait()
    own_rows.wait()


def gather_call(idx, tile, strip, slab):
    anywhere = pl.BlockSpec(memory_space=pl.ANY)
    vmem = pl.BlockSpec(memory_space=pltpu.VMEM)
    dma = pltpu.SemaphoreType.DMA
    return pl.pallas_call(
        gather_kernel,
        out_shape=(
            jax.ShapeDtypeStruct((STEPS, B, B), F32),
            jax.ShapeDtypeStruct((STEPS, B, B), F32),
            jax.ShapeDtypeStruct((STEPS, W, B), F32),
            jax.ShapeDtypeStruct((16, W, B), F32),
            jax.ShapeDtypeStruct((8, 1024, B), F32),
        ),
        in_specs=[pl.BlockSpec(memory_space=pltpu.SMEM), vmem, anywhere, anywhere],
        out_specs=(vmem, vmem, vmem, anywhere, anywhere),
        scratch_shapes=[
            pltpu.VMEM((16, 8, B), F32),
            pltpu.VMEM((STEPS, 8, B), F32),
            pltpu.VMEM((8, STEPS, 8, B), F32),
            pltpu.VMEM((STEPS, 16, 8, W), F32),
            pltpu.VMEM((16, B, B), F32),
            pltpu.VMEM((W, B), F32),
            dma((16,)), dma((16,)), dma((16,)), dma((16,)), dma((8,)), dma((8,)),
            dma((Ring.COUNT,)), dma((Ring.COUNT,)), dma, dma,
            dma((Ring.COUNT,)), dma((Ring.COUNT,)), dma((8,)), dma((8,)), dma((3,)),
        ],
        compiler_params=pltpu.CompilerParams(
            collective_id=0, has_side_effects=True, vmem_limit_bytes=56 * 2**20
        ),
        name="gather_factor",
    )(idx, tile, strip, slab)


def split(x):
    high = x.astype(BF16)
    return high, (x - high.astype(F32)).astype(BF16)


def dot3(a, b, dims):
    dot = functools.partial(lax.dot_general, dimension_numbers=dims, preferred_element_type=F32)
    return dot(a[0], b[0]) + (dot(a[0], b[1]) + dot(a[1], b[0]))


PAIR = 2 * B


def update_kernel(
    info, c0, c1, c2, c3, c4, c5, upper, inverse, lower, rows_ref, a_ref, o_ref,
    left_h, left_l, right_h, right_l,
):
    m = pl.program_id(0)
    k0, p, q = info[0], info[1], info[2]

    @pl.when(m == 0)
    def _():
        for b, c_ref in enumerate((c0, c1, c2, c3, c4, c5)):
            x = c_ref[0]
            if b:
                known = (left_h[:, : b * B], left_l[:, : b * B])
                strip = jnp.concatenate([lower[a, b * B : (b + 1) * B, :] for a in range(b)], 1)
                x = x - dot3(known, split(strip), NT)
            x = dot3(split(x), split(inverse[b]), NT)
            high, low = split(x)
            left_h[:, b * B : (b + 1) * B] = high
            left_l[:, b * B : (b + 1) * B] = low

    first = 2 * m * 8 + q
    second = first + 8
    last = k0 + STEPS - 1

    @pl.when(second > last)
    def _():
        for b in range(STEPS):
            x = jnp.concatenate(
                [rows_ref[0, b * B : (b + 1) * B, :], rows_ref[1, b * B : (b + 1) * B, :]], 1
            )
            if b:
                known = (right_h[: b * B, :], right_l[: b * B, :])
                strip = jnp.concatenate([lower[a, b * B : (b + 1) * B, :] for a in range(b)], 1)
                x = x - dot3(split(strip), known, NN)
            x = dot3(split(inverse[b]), split(x), NN)
            high, low = split(x)
            right_h[b * B : (b + 1) * B, :] = high
            right_l[b * B : (b + 1) * B, :] = low

    for part in range(4):

        @pl.when(m // 2 == part)
        def _():
            top = part * PAIR
            if part:
                o_ref[:top, :] = a_ref[:top, :]

            @pl.when(second > last)
            def _():
                count = 1024 - top
                update = dot3(
                    (left_h[top:, :], left_l[top:, :]), (right_h[...], right_l[...]), NN
                )
                row = (lax.broadcasted_iota(jnp.int32, (count, PAIR), 0) + top) // B * 16 + p
                col = lax.broadcasted_iota(jnp.int32, (count, PAIR), 1) // B * 8 + first
                keep = (row >= col) & (col > last)
                o_ref[top:, :] = a_ref[top:, :] - jnp.where(keep, update, 0.0)

            @pl.when(second <= last)
            def _():
                o_ref[top:, :] = a_ref[top:, :]

    for side in range(2):
        col = first + 8 * side
        lanes = slice(side * B, (side + 1) * B)
        for b in range(STEPS):

            @pl.when(col == k0 + b)
            def _():
                solved = left_h[:, b * B : (b + 1) * B].astype(F32) + left_l[
                    :, b * B : (b + 1) * B
                ].astype(F32)
                row = lax.broadcasted_iota(jnp.int32, (1024, B), 0) // B * 16 + p
                factor = jnp.concatenate([jnp.transpose(upper[b])] * 8, 0)
                o_ref[:, lanes] = jnp.where(
                    row > col, solved, jnp.where(row == col, factor, a_ref[:, lanes])
                )


def update_call(info, upper, inverse, lower, rout, cout, working):
    def column(b):
        return pl.BlockSpec((1, 1024, B), lambda m, info: (lax.rem(info[0] + b, 8), 0, 0))

    def fixed(shape):
        return pl.BlockSpec(shape, lambda m, info: (0,) * len(shape))

    return pl.pallas_call(
        update_kernel,
        out_shape=jax.ShapeDtypeStruct(working.shape, F32),
        grid_spec=pltpu.PrefetchScalarGridSpec(
            num_scalar_prefetch=1,
            grid=(8,),
            in_specs=[column(b) for b in range(STEPS)]
            + [
                fixed((STEPS, B, B)),
                fixed((STEPS, B, B)),
                fixed((STEPS, W, B)),
                pl.BlockSpec((2, W, B), lambda m, info: (m, 0, 0)),
                pl.BlockSpec((1024, PAIR), lambda m, info: (0, m)),
            ],
            out_specs=pl.BlockSpec((1024, PAIR), lambda m, info: (0, m)),
            scratch_shapes=[
                pltpu.VMEM((1024, W), BF16),
                pltpu.VMEM((1024, W), BF16),
                pltpu.VMEM((W, PAIR), BF16),
                pltpu.VMEM((W, PAIR), BF16),
            ],
        ),
        compiler_params=pltpu.CompilerParams(vmem_limit_bytes=56 * 2**20),
        name="update",
    )(info, *([cout] * STEPS), upper, inverse, lower, rout, working)


def local(working, step):
    p = lax.axis_index("row").astype(jnp.int32)
    q = lax.axis_index("col").astype(jnp.int32)
    k0 = step[0]
    turns = jnp.arange(STEPS, dtype=jnp.int32)
    idx = jnp.concatenate([(k0 + turns) % 16, (k0 + turns) % 8])
    t = jnp.minimum((k0 + (p - k0) % 16) // 16, 7)
    c = jnp.minimum((k0 + (q - k0) % 8) // 8, 15)
    strip = lax.dynamic_slice(working, (t * B, 0), (B, 2048))
    slab = lax.dynamic_slice(working, (0, c * B), (1024, B))
    tile = lax.dynamic_slice(working, (t * B, c * B), (B, B))
    upper, inverse, lower, rout, cout = gather_call(idx, tile, strip, slab)
    info = jnp.stack([k0, p, q])
    return update_call(info, upper, inverse, lower, rout, cout, working)


def solution(mesh):
    placed = (P("row", "col"), P())
    return jax.shard_map(
        local, mesh=mesh, in_specs=placed, out_specs=P("row", "col"), check_vma=False
    )
```

time: 1680 us -> 141 us (0.08)
  waiting for transfers between devices: 1360 us -> 0 us
  other arithmetic: 165 us -> 1.31 us
  Pallas kernels: 0 us -> 133 us
  matrix products: 76.1 us -> 0 us
  local copies, waits for them, and re-layouts: 49.2 us -> 5.67 us
    psum x18 -> x0, waiting for transfers between devices: 1360 us -> none  [the longest x12 845 us: broadcast(): return lax.psum(block, axis)]
    another operation x30 -> x1, other arithmetic: 138 us -> 0.64 us  [local(): info = jnp.stack([k0, p, q])]
    pallas_call x0 -> x2, Pallas kernels: none -> 133 us  [the longest x1 93.6 us: gather_call(): pl.pallas_call(gather_kernel, out_shape=(jax.ShapeDtypeStruct((STEPS, B,...]
    dot_general x6 -> x0, matrix products: 61.3 us -> none  [local(): update = jnp.dot(panel_here, panel_cols.T, precision=lax.Precision.HIGHEST)]
    unnamed x11 -> x0, local copies, waits for them, and re-layouts: 26.2 us -> none
  transfers between devices with their start and end apart: 18 -> 0, of which waited for: 18 -> 0; matrix products, arithmetic and copies ran while one was open for 0% -> 0% of each run, Pallas kernels for 0% -> 0%
where the time goes in v1:
time: 141 us; the launch traced here: 140 us
  Pallas kernels  133 us (94%)
  local copies, waits for them, and re-layouts  5.67 us (4%)
    pallas_call x1, Pallas kernels, gather_call(): pl.pallas_call(gather_kernel, out_shape=(jax.ShapeDtypeStruct((STEPS, B,...  93.6 us
    pallas_call x1, Pallas kernels, update_call(): pl.pallas_call(update_kernel, out_shape=jax.ShapeDtypeStruct(working.shap...  39.1 us

profile of v1, /device:TPU:0, one launch (start us, length us, event | category | flops | bytes accessed | tf_op | source)
XLA Modules:
  0.0 140.5 jit_solution(8835427608622658685)
XLA Ops:
  0.7 0.6 pad_add_fusion.info
  1.4 0.7 pad_add_fusion.1.idx
  2.1 1.5 %dynamic_slice.9.tile = f32[128,128]{1,0:T(8,128)} dynamic-slice(f32[1024,2048]{1,0:T(8,128)} %a_ref.1, s32[]{:T(128)S(6)} %select_n.40, s32[]{:T(128)S(6)} %select_n.43), dynamic_slice_sizes={128,128} | dynamic-slice | bytes 131076 | tf_op jit(solution)/shard_map/dynamic_slice | solution.py:487
  3.5 1.9 %constant_dynamic-slice_fusion.slab = f32[1024,128]{1,0:T(8,128)} fusion(f32[1024,2048]{1,0:T(8,128)} %a_ref.1, s32[]{:T(128)S(6)} %select_n.43), kind=kLoop, calls=%fused_computation.7 | loop fusion | bytes 1048580 | tf_op jit(solution)/shard_map/dynamic_slice | solution.py:486
  5.4 2.3 %constant_dynamic-slice_fusion.1.strip = f32[128,2048]{1,0:T(8,128)} fusion(f32[1024,2048]{1,0:T(8,128)} %a_ref.1, s32[]{:T(128)S(6)} %select_n.40), kind=kLoop, calls=%fused_computation.8 | loop fusion | bytes 2097156 | tf_op jit(solution)/shard_map/dynamic_slice | solution.py:485
  7.7 93.6 %gather_factor.1 = (f32[6,128,128]{2,1,0:T(8,128)}, f32[6,128,128]{2,1,0:T(8,128)}, f32[6,768,128]{2,1,0:T(8,128)}, f32[16,768,128]{2,1,0:T(8,128)}, f32[8,1024,128]{2,1,0:T(8,128)}) custom-call(s32[12]{0:T(128)} %pad_add_fusion.1.idx, f32[128,128]{1,0:T(8,128)} %dynamic_slice.9.tile, f32[128,2048]{1,0:T(8,128)} %constant_dynamic-slice_fusion.1.strip, ...), custom_call_target="tpu_custom_call" | custom-call | tf_op jit(solution)/shard_map/gather_factor/pallas_call | solution.py:322
  101.4 39.1 %update.1 = f32[1024,2048]{1,0:T(8,128)} custom-call(s32[3]{0:T(128)} %pad_add_fusion.info, f32[8,1024,128]{2,1,0:T(8,128)} %get-tuple-element.10.c0.c1.c2.c3.c4.c5, f32[8,1024,128]{2,1,0:T(8,128)} %get-tuple-element.10.c0.c1.c2.c3.c4.c5, f32[8,1024,128]{2,1,0:T(8,128)} %get-tuple-element.10.c0.c1.c2.c3.c4.c5, ...), custom_call_target="tpu_custom_call" | custom-call | tf_op jit(solution)/shard_map/update/pallas_call | solution.py:450
  (1 shorter events, 0.0 us)

commit v2 on v1

--- a/solution.py
+++ b/solution.py
@@ -129,21 +129,36 @@
 
 
 def gather_kernel(
-    idx, tile, strip, slab,
-    upper_o, inverse_o, lower_o, rout, cout,
-    dbuf, dcol, dcg, whole, rbuf, bst,
+    step_ref, working,
+    upper_o, inverse_o, rout, cout,
+    staged, tile, strip, slab, dbuf, dcol, dcg, whole, rbuf, bst,
     d1s, d1r, a1s, a1r, d2s, d2r, d3s, d3r, sibs, sibr, rs, rr, cs, cr, local,
 ):
     p, q = lax.axis_index("row"), lax.axis_index("col")
     core, y = lax.rem(q, 2), q // 2
     sibling = q + 1 - 2 * core
-
+    k0 = step_ref[0]
+
+    stages = [
+        pltpu.make_async_copy(
+            working.at[:, :, pl.ds(j * B, B)], staged.at[j], local.at[2 + j]
+        )
+        for j in range(16)
+    ]
+    for stage in stages:
+        stage.start()
     barrier = pltpu.get_barrier_semaphore()
     for d in range(1, 16):
         pl.semaphore_signal(barrier, inc=1, device_id=(lax.rem(p + d, 16), q), device_id_type=MESH)
     for d in range(1, 8):
         pl.semaphore_signal(barrier, inc=1, device_id=(p, lax.rem(q + d, 8)), device_id_type=MESH)
     pl.semaphore_wait(barrier, 22)
+    for stage in stages:
+        stage.wait()
+
+    t = jnp.minimum(lax.div(k0 + lax.rem(p - k0 + 128, 16), 16), 7)
+    c = jnp.minimum(lax.div(k0 + lax.rem(q - k0 + 128, 8), 8), 15)
+    tile[...] = staged[c, t]
 
     def remote(src, dst, send, recv, device):
         return pltpu.make_async_remote_copy(
@@ -158,8 +173,7 @@
 
     def piece(d, slot):
         to = lax.rem(p + d, 16)
-        columns = pl.ds(pl.multiple_of(B * to, B), B)
-        return remote(strip.at[:, columns], rbuf.at[slot], a1s.at[d], a1r.at[d], (to, q))
+        return remote(strip.at[to], rbuf.at[slot], a1s.at[d], a1r.at[d], (to, q))
 
     def spread(d, slot):
         to = lax.rem(q + d, 8)
@@ -167,19 +181,19 @@
 
     for d in range(1, 16):
         diag(d, p).start()
+    for j in range(16):
+        strip[j] = staged[j, t]
     for d in range(1, 16):
         piece(d, p).start()
-    own_piece = pltpu.make_async_copy(
-        strip.at[:, pl.ds(pl.multiple_of(B * p, B), B)], rbuf.at[p], local.at[0]
-    )
-    own_piece.start()
+    rbuf[p] = strip[p]
+    slab[...] = staged[c].reshape(1024, B)
     own_slab = pltpu.make_async_copy(slab, cout.at[q], local.at[1])
     own_slab.start()
     dbuf[p] = tile[pl.ds(pl.multiple_of(8 * p, 8), 8), :]
     for d in range(1, 16):
         diag(d, lax.rem(p + 16 - d, 16)).wait_recv()
     for s in range(STEPS):
-        block = dbuf[idx[s]]
+        block = dbuf[lax.rem(k0 + s, 16)]
         dcol[s] = block
         dcg[q, s] = block
     for d in range(1, 8):
@@ -233,7 +247,7 @@
         spread(d, lax.rem(q + 8 - d, 8)).wait_recv()
     half = pl.ds(3 * core, 3)
     for b in range(STEPS):
-        whole[half, p, :, b * B : (b + 1) * B] = dcg[idx[STEPS + b], half]
+        whole[half, p, :, b * B : (b + 1) * B] = dcg[lax.rem(k0 + b, 8), half]
 
     def diag_view(block, part):
         if part is None:
@@ -248,23 +262,23 @@
     diag_ring.tick(0)
     columns_tick(0)
 
-    own_piece.wait()
     for d in range(1, 16):
         piece(d, lax.rem(p + 16 - d, 16)).wait_recv()
     for s in range(STEPS):
-        bst[s * B : (s + 1) * B, :] = rbuf[idx[s]]
-    own_rows = pltpu.make_async_copy(bst, rout.at[p], local.at[2])
+        bst[s * B : (s + 1) * B, :] = rbuf[lax.rem(k0 + s, 16)]
+    own_rows = pltpu.make_async_copy(bst, rout.at[p], local.at[0])
     own_rows.start()
+    row_ring.tick(0)
     diag_ring.tick(1)
     diag_ring.tick(2)
     diag_ring.tick(3)
-    row_ring.tick(0)
+    columns_tick(1)
     diag_ring.tick(4)
     other = pl.ds(3 - 3 * core, 3)
     to_sibling = remote(whole.at[half], whole.at[half], sibs, sibr, (p, sibling))
     from_sibling = remote(whole.at[other], whole.at[other], sibs, sibr, (p, sibling))
     to_sibling.start()
-    columns_tick(1)
+    row_ring.tick(1)
     from_sibling.wait_recv()
     to_sibling.wait_send()
     diag_ring.finish()
@@ -273,30 +287,39 @@
         here = pl.ds(pl.multiple_of(k * B, B), B)
         upper, inverse = factor_tile(whole[k, :, :, here].reshape(B, B))
         upper_o[k] = upper
-        inverse_o[k] = inverse
+        dot = functools.partial(
+            lax.dot_general, precision=HIGHEST, preferred_element_type=F32
+        )
         for i in range(STEPS):
 
             @pl.when(k == i)
             def _():
+                at = slice(i * B, (i + 1) * B)
+                inverse_o[at, at] = inverse
+                if i:
+                    known = whole[i, :, :, : i * B].reshape(B, i * B)
+                    inverse_o[at, : i * B] = dot(inverse, known, NN)
                 if i < STEPS - 1:
                     left = STEPS - 1 - i
-                    below = whole[i + 1 :, :, :, i * B : (i + 1) * B].reshape(left * B, B)
-                    solved = lax.dot_general(
-                        below, inverse_o[i], NT, precision=HIGHEST, preferred_element_type=F32
-                    )
-                    lower_o[i, (i + 1) * B :, :] = solved
-                    update = lax.dot_general(
-                        solved, solved, NT, precision=HIGHEST, preferred_element_type=F32
-                    )
+                    inverse_o[at, (i + 1) * B :] = jnp.zeros((B, left * B), F32)
+                    below = whole[i + 1 :, :, :, at].reshape(left * B, B)
+                    solved = dot(below, inverse, NT)
+                    update = dot(solved, solved, NT)
                     whole[i + 1 :, :, :, (i + 1) * B :] = whole[
                         i + 1 :, :, :, (i + 1) * B :
                     ] - update.reshape(left, 16, 8, left * B)
+                    update = dot(solved, inverse_o[at, : (i + 1) * B], NN)
+                    update = update.reshape(left, 16, 8, (i + 1) * B)
+                    if i:
+                        whole[i + 1 :, :, :, : i * B] = (
+                            whole[i + 1 :, :, :, : i * B] - update[:, :, :, : i * B]
+                        )
+                    whole[i + 1 :, :, :, at] = -update[:, :, :, i * B :]
                 if i == 0:
-                    row_ring.tick(1)
                     columns_tick(2)
-                if i == 2:
+                if i == 1:
                     row_ring.tick(2)
-                if i == 4:
+                if i == 3:
                     row_ring.tick(3)
                 if i == 5:
                     row_ring.tick(4)
@@ -315,7 +338,7 @@
     own_rows.wait()
 
 
-def gather_call(idx, tile, strip, slab):
+def gather_call(step, working):
     anywhere = pl.BlockSpec(memory_space=pl.ANY)
     vmem = pl.BlockSpec(memory_space=pltpu.VMEM)
     dma = pltpu.SemaphoreType.DMA
@@ -323,14 +346,17 @@
         gather_kernel,
         out_shape=(
             jax.ShapeDtypeStruct((STEPS, B, B), F32),
-            jax.ShapeDtypeStruct((STEPS, B, B), F32),
-            jax.ShapeDtypeStruct((STEPS, W, B), F32),
+            jax.ShapeDtypeStruct((W, W), F32),
             jax.ShapeDtypeStruct((16, W, B), F32),
             jax.ShapeDtypeStruct((8, 1024, B), F32),
         ),
-        in_specs=[pl.BlockSpec(memory_space=pltpu.SMEM), vmem, anywhere, anywhere],
-        out_specs=(vmem, vmem, vmem, anywhere, anywhere),
+        in_specs=[pl.BlockSpec(memory_space=pltpu.SMEM), anywhere],
+        out_specs=(vmem, vmem, anywhere, anywhere),
         scratch_shapes=[
+            pltpu.VMEM((16, 8, B, B), F32),
+            pltpu.VMEM((B, B), F32),
+            pltpu.VMEM((16, B, B), F32),
+            pltpu.VMEM((1024, B), F32),
             pltpu.VMEM((16, 8, B), F32),
             pltpu.VMEM((STEPS, 8, B), F32),
             pltpu.VMEM((8, STEPS, 8, B), F32),
@@ -339,13 +365,13 @@
             pltpu.VMEM((W, B), F32),
             dma((16,)), dma((16,)), dma((16,)), dma((16,)), dma((8,)), dma((8,)),
             dma((Ring.COUNT,)), dma((Ring.COUNT,)), dma, dma,
-            dma((Ring.COUNT,)), dma((Ring.COUNT,)), dma((8,)), dma((8,)), dma((3,)),
+            dma((Ring.COUNT,)), dma((Ring.COUNT,)), dma((8,)), dma((8,)), dma((18,)),
         ],
         compiler_params=pltpu.CompilerParams(
             collective_id=0, has_side_effects=True, vmem_limit_bytes=56 * 2**20
         ),
         name="gather_factor",
-    )(idx, tile, strip, slab)
+    )(step, working.reshape(8, B, 2048))
 
 
 def split(x):
@@ -362,24 +388,22 @@
 
 
 def update_kernel(
-    info, c0, c1, c2, c3, c4, c5, upper, inverse, lower, rows_ref, a_ref, o_ref,
-    left_h, left_l, right_h, right_l,
+    info, c0, c1, c2, c3, c4, c5, upper, inverse, rows_ref, a_ref, o_ref,
+    inverse_h, inverse_l, left_h, left_l, right_h, right_l,
 ):
     m = pl.program_id(0)
-    k0, p, q = info[0], info[1], info[2]
+    k0, p, q = info[0], lax.axis_index("row"), lax.axis_index("col")
 
     @pl.when(m == 0)
     def _():
-        for b, c_ref in enumerate((c0, c1, c2, c3, c4, c5)):
-            x = c_ref[0]
-            if b:
-                known = (left_h[:, : b * B], left_l[:, : b * B])
-                strip = jnp.concatenate([lower[a, b * B : (b + 1) * B, :] for a in range(b)], 1)
-                x = x - dot3(known, split(strip), NT)
-            x = dot3(split(x), split(inverse[b]), NT)
-            high, low = split(x)
-            left_h[:, b * B : (b + 1) * B] = high
-            left_l[:, b * B : (b + 1) * B] = low
+        inverse_h[...], inverse_l[...] = split(inverse[...])
+        parts = [split(c_ref[0]) for c_ref in (c0, c1, c2, c3, c4, c5)]
+        for b in range(0, STEPS, 2):
+            end = (b + 2) * B
+            at = slice(b * B, end)
+            known = [jnp.concatenate([part[i] for part in parts[: b + 2]], 1) for i in range(2)]
+            x = dot3(known, (inverse_h[at, :end], inverse_l[at, :end]), NT)
+            left_h[:, at], left_l[:, at] = split(x)
 
     first = 2 * m * 8 + q
     second = first + 8
@@ -387,18 +411,12 @@
 
     @pl.when(second > last)
     def _():
-        for b in range(STEPS):
-            x = jnp.concatenate(
-                [rows_ref[0, b * B : (b + 1) * B, :], rows_ref[1, b * B : (b + 1) * B, :]], 1
-            )
-            if b:
-                known = (right_h[: b * B, :], right_l[: b * B, :])
-                strip = jnp.concatenate([lower[a, b * B : (b + 1) * B, :] for a in range(b)], 1)
-                x = x - dot3(split(strip), known, NN)
-            x = dot3(split(inverse[b]), split(x), NN)
-            high, low = split(x)
-            right_h[b * B : (b + 1) * B, :] = high
-            right_l[b * B : (b + 1) * B, :] = low
+        x = split(jnp.concatenate([rows_ref[0], rows_ref[1]], 1))
+        for b in range(0, STEPS, 2):
+            end = (b + 2) * B
+            at = slice(b * B, end)
+            y = dot3((inverse_h[at, :end], inverse_l[at, :end]), (x[0][:end], x[1][:end]), NN)
+            right_h[at, :], right_l[at, :] = split(y)
 
     for part in range(4):
 
@@ -440,7 +458,7 @@
                 )
 
 
-def update_call(info, upper, inverse, lower, rout, cout, working):
+def update_call(step, upper, inverse, rout, cout, working):
     def column(b):
         return pl.BlockSpec((1, 1024, B), lambda m, info: (lax.rem(info[0] + b, 8), 0, 0))
 
@@ -456,13 +474,14 @@
             in_specs=[column(b) for b in range(STEPS)]
             + [
                 fixed((STEPS, B, B)),
-                fixed((STEPS, B, B)),
-                fixed((STEPS, W, B)),
+                fixed((W, W)),
                 pl.BlockSpec((2, W, B), lambda m, info: (m, 0, 0)),
                 pl.BlockSpec((1024, PAIR), lambda m, info: (0, m)),
             ],
             out_specs=pl.BlockSpec((1024, PAIR), lambda m, info: (0, m)),
             scratch_shapes=[
+                pltpu.VMEM((W, W), BF16),
+                pltpu.VMEM((W, W), BF16),
                 pltpu.VMEM((1024, W), BF16),
                 pltpu.VMEM((1024, W), BF16),
                 pltpu.VMEM((W, PAIR), BF16),
@@ -471,23 +490,12 @@
         ),
         compiler_params=pltpu.CompilerParams(vmem_limit_bytes=56 * 2**20),
         name="update",
-    )(info, *([cout] * STEPS), upper, inverse, lower, rout, working)
+    )(step, *([cout] * STEPS), upper, inverse, rout, working)
 
 
 def local(working, step):
-    p = lax.axis_index("row").astype(jnp.int32)
-    q = lax.axis_index("col").astype(jnp.int32)
-    k0 = step[0]
-    turns = jnp.arange(STEPS, dtype=jnp.int32)
-    idx = jnp.concatenate([(k0 + turns) % 16, (k0 + turns) % 8])
-    t = jnp.minimum((k0 + (p - k0) % 16) // 16, 7)
-    c = jnp.minimum((k0 + (q - k0) % 8) // 8, 15)
-    strip = lax.dynamic_slice(working, (t * B, 0), (B, 2048))
-    slab = lax.dynamic_slice(working, (0, c * B), (1024, B))
-    tile = lax.dynamic_slice(working, (t * B, c * B), (B, B))
-    upper, inverse, lower, rout, cout = gather_call(idx, tile, strip, slab)
-    info = jnp.stack([k0, p, q])
-    return update_call(info, upper, inverse, lower, rout, cout, working)
+    upper, inverse, rout, cout = gather_call(step, working)
+    return update_call(step, upper, inverse, rout, cout, working)
 
 
 def solution(mesh):

time: 141 us -> 108 us (0.77)
  Pallas kernels: 133 us -> 106 us
  local copies, waits for them, and re-layouts: 5.67 us -> 0 us
    pallas_call x1, Pallas kernels: 39.1 us -> 17.4 us  [update_call(): pl.pallas_call(update_kernel, out_shape=jax.ShapeDtypeStruct(working.shap...]
    dynamic_slice x3 -> x0, local copies, waits for them, and re-layouts: 5.67 us -> none  [the longest x1 2.29 us: local(): strip = lax.dynamic_slice(working, (t * B, 0), (B, 2048))]
    pallas_call x1, Pallas kernels: 93.6 us -> 88.6 us  [gather_call(): pl.pallas_call(gather_kernel, out_shape=(jax.ShapeDtypeStruct((STEPS, B,...]
where the time goes in v2:
time: 108 us; the launch traced here: 107 us
  Pallas kernels  106 us (98%)
    pallas_call x1, Pallas kernels, gather_call(): pl.pallas_call(gather_kernel, out_shape=(jax.ShapeDtypeStruct((STEPS, B,...  88.6 us
    pallas_call x1, Pallas kernels, update_call(): pl.pallas_call(update_kernel, out_shape=jax.ShapeDtypeStruct(working.shap...  17.4 us

profile of v2, /device:TPU:0, one launch (start us, length us, event | category | flops | bytes accessed | tf_op | source)
XLA Modules:
  0.0 106.6 jit_solution(15176678005021724392)
XLA Ops:
  0.7 88.6 %gather_factor.1 = (f32[6,128,128]{2,1,0:T(8,128)}, f32[768,768]{1,0:T(8,128)}, f32[16,768,128]{2,1,0:T(8,128)}, f32[8,1024,128]{2,1,0:T(8,128)}) custom-call(s32[1]{0:T(128)S(6)} %copy.3.step_ref.info, f32[8,128,2048]{2,1,0:T(8,128)} %bitcast.1), custom_call_target="tpu_custom_call" | custom-call | tf_op jit(solution)/shard_map/gather_factor/pallas_call | solution.py:345
  89.2 17.4 %update.1 = f32[1024,2048]{1,0:T(8,128)} custom-call(s32[1]{0:T(128)S(6)} %copy.3.step_ref.info, f32[8,1024,128]{2,1,0:T(8,128)} %get-tuple-element.9.c0.c1.c2.c3.c4.c5, f32[8,1024,128]{2,1,0:T(8,128)} %get-tuple-element.9.c0.c1.c2.c3.c4.c5, f32[8,1024,128]{2,1,0:T(8,128)} %get-tuple-element.9.c0.c1.c2.c3.c4.c5, ...), custom_call_target="tpu_custom_call" | custom-call | tf_op jit(solution)/shard_map/update/pallas_call | solution.py:468

commit v3 on v2

--- a/solution.py
+++ b/solution.py
@@ -10,6 +10,7 @@
 B = 128
 STEPS = 6
 W = B * STEPS
+LOWER = [(a, b) for a in range(STEPS) for b in range(a + 1)]
 F32 = jnp.float32
 BF16 = jnp.bfloat16
 MESH = pl.DeviceIdType.MESH
@@ -18,34 +19,60 @@
 NN = (((1,), (0,)), ((), ()))
 
 
-def factor_tile(tile):
-    chunk = 8
-    rest = tile
-    other = (
-        lax.broadcasted_iota(jnp.int32, (B, B), 0) == lax.broadcasted_iota(jnp.int32, (B, B), 1)
-    ).astype(F32)
+def factor_tile(tile, hook):
+    sub = lax.broadcasted_iota(jnp.int32, (8, B), 0)
+    lane = lax.broadcasted_iota(jnp.int32, (8, B), 1)
+    lanes = lax.broadcasted_iota(jnp.int32, (B, B), 1)
+
+    def spread(x, first):
+        return [jnp.broadcast_to(x[:, first + i : first + i + 1], x.shape) for i in range(8)]
+
+    head, rest = tile[:8], tile[8:]
+    held = spread(head, 0)
     uppers, inverses = [], []
-    for first in range(0, B, chunk):
-        rows = B - first
-        row = lax.broadcasted_iota(jnp.int32, (rows, B), 0)
-        coefs = [
-            jnp.broadcast_to(rest[:, first + i : first + i + 1], (rows, B)) for i in range(chunk)
-        ]
+    for first in range(0, B, 8):
+        if first == B // 2:
+            hook()
+        more = first + 8 < B
+        if more:
+            coefs = spread(rest, first)
+            head_next = spread(head, first + 8)
+            rest_next = spread(rest[:8], first + 8)
+            at = lanes[: B - first - 8]
+            rest = jnp.where((at >= first) & (at < first + 8), 0.0, rest)
+        inside = (lane >= first) & (lane < first + 8)
+        head = jnp.where(inside, jnp.where(lane - first == sub, 1.0, 0.0), head)
         scales = []
-        for j in range(chunk):
-            scale = lax.rsqrt(coefs[j][j : j + 1, :])
-            scales.append(scale)
-            factor = jnp.where(row > j, coefs[j] * (scale * scale), 0.0)
-            rest = rest - factor * rest[j : j + 1, :]
-            other = other - factor * other[j : j + 1, :]
-            for i in range(j + 1, chunk):
-                coefs[i] = coefs[i] - factor * coefs[i][j : j + 1, :]
+        for j in range(8):
+            pivot = held[j][j : j + 1]
+            inverse = 1.0 / pivot
+            scales.append(lax.rsqrt(pivot))
+            factor = jnp.where(sub > j, held[j] * inverse, 0.0)
+            row = head[j : j + 1]
+            cross = [held[i][j : j + 1] for i in range(8)]
+            for i in range(j + 1, 8):
+                held[i] = held[i] - factor * cross[i]
+            if more:
+                further = [head_next[i][j : j + 1] for i in range(8)]
+            head = head - factor * row
+            if more:
+                below = coefs[j] * inverse
+                for i in range(j + 1, 8):
+                    coefs[i] = coefs[i] - below * cross[i]
+                rest = rest - below * row
+                for i in range(8):
+                    head_next[i] = head_next[i] - factor * further[i]
+                    rest_next[i] = rest_next[i] - below[:8] * further[i]
         scale = jnp.concatenate(scales, 0)
-        sub = lax.broadcasted_iota(jnp.int32, (chunk, B), 0)
-        lane = lax.broadcasted_iota(jnp.int32, (chunk, B), 1)
-        uppers.append(jnp.where(lane >= first + sub, rest[:chunk] * scale, 0.0))
-        inverses.append(other[:chunk] * scale)
-        rest, other = rest[chunk:], other[chunk:]
+        done = head * scale
+        upper = jnp.where(lane >= first + 8, done, 0.0)
+        for i in range(8):
+            upper = jnp.where((lane == first + i) & (sub <= i), held[i] * scale, upper)
+        uppers.append(upper)
+        inverses.append(jnp.where(lane < first + 8, done, 0.0))
+        if more:
+            held = rest_next
+            head, rest = rest[:8], rest[8:]
     return jnp.concatenate(uppers, 0), jnp.concatenate(inverses, 0)
 
 
@@ -131,8 +158,8 @@
 def gather_kernel(
     step_ref, working,
     upper_o, inverse_o, rout, cout,
-    staged, tile, strip, slab, dbuf, dcol, dcg, whole, rbuf, bst,
-    d1s, d1r, a1s, a1r, d2s, d2r, d3s, d3r, sibs, sibr, rs, rr, cs, cr, local,
+    staged, tile, strip, slab, dbuf, dcol, dcg, dall, packed, whole, rbuf, bst,
+    d1s, d1r, a1s, a1r, d2s, d2r, d3s, d3r, sibs, sibr, rs, rr, rs2, rr2, cs, cr, local,
 ):
     p, q = lax.axis_index("row"), lax.axis_index("col")
     core, y = lax.rem(q, 2), q // 2
@@ -223,8 +250,8 @@
         if tick == 0:
             along(*along_messages[0], False).start()
             along(*along_messages[1], False).start()
+        elif tick == 1:
             across(*across_messages[0], False).start()
-        elif tick == 1:
             along(*along_messages[0], True).wait_recv()
             along(*along_messages[1], True).wait_recv()
             along(*along_messages[2], False).start()
@@ -245,21 +272,30 @@
 
     for d in range(1, 8):
         spread(d, lax.rem(q + 8 - d, 8)).wait_recv()
-    half = pl.ds(3 * core, 3)
-    for b in range(STEPS):
-        whole[half, p, :, b * B : (b + 1) * B] = dcg[lax.rem(k0 + b, 8), half]
-
-    def diag_view(block, part):
-        if part is None:
-            return whole.at[half, block]
-        return whole.at[half, block, :, pl.ds(384 * part, 384)]
-
-    def row_view(block, part):
-        return rout.at[block] if part is None else rout.at[block, pl.ds(384 * part, 384), :]
-
-    diag_ring = Ring(p, q, diag_view, None, d3s, d3r)
-    row_ring = Ring(p, q, row_view, bst, rs, rr)
-    diag_ring.tick(0)
+    for n, (a, b) in enumerate(LOWER):
+        dall[n] = dcg[lax.rem(k0 + b, 8), a]
+    dall[len(LOWER)] = jnp.zeros((8, B), F32)
+    half = pl.ds(11 * core, 11)
+    packed[p, half] = dall[half]
+
+    def block(d, slot):
+        mine = packed.at[slot, half]
+        return remote(mine, mine, d3s.at[d], d3r.at[d], (lax.rem(p + d, 16), q))
+
+    def row_view(stream):
+        def view(block, part):
+            if part is None:
+                return rout.at[block, pl.ds(384 * stream, 384), :]
+            return rout.at[block, pl.ds(384 * stream + 192 * part, 192), :]
+
+        return view
+
+    streams = [
+        Ring(p, q, row_view(0), bst.at[:384], rs, rr),
+        Ring(p, q, row_view(1), bst.at[384:], rs2, rr2),
+    ]
+    for d in range(1, 16):
+        block(d, p).start()
     columns_tick(0)
 
     for d in range(1, 16):
@@ -268,24 +304,41 @@
         bst[s * B : (s + 1) * B, :] = rbuf[lax.rem(k0 + s, 16)]
     own_rows = pltpu.make_async_copy(bst, rout.at[p], local.at[0])
     own_rows.start()
-    row_ring.tick(0)
-    diag_ring.tick(1)
-    diag_ring.tick(2)
-    diag_ring.tick(3)
-    columns_tick(1)
-    diag_ring.tick(4)
-    other = pl.ds(3 - 3 * core, 3)
-    to_sibling = remote(whole.at[half], whole.at[half], sibs, sibr, (p, sibling))
-    from_sibling = remote(whole.at[other], whole.at[other], sibs, sibr, (p, sibling))
+    streams[0].tick(0)
+    streams[1].tick(0)
+    for d in range(1, 16):
+        block(d, lax.rem(p + 16 - d, 16)).wait_recv()
+    other = pl.ds(11 - 11 * core, 11)
+    to_sibling = remote(packed.at[:, half], packed.at[:, half], sibs, sibr, (p, sibling))
+    from_sibling = remote(packed.at[:, other], packed.at[:, other], sibs, sibr, (p, sibling))
     to_sibling.start()
-    row_ring.tick(1)
+    streams[0].tick(1)
     from_sibling.wait_recv()
-    to_sibling.wait_send()
-    diag_ring.finish()
+    for n, (a, b) in enumerate(LOWER):
+        whole[a, :, :, b * B : (b + 1) * B] = packed[:, n]
+
+    def run(ring_tick, first, column_tick, second):
+        ring_tick(first)
+        column_tick(second)
+
+    ticks = {
+        (0, 1): lambda: run(streams[1].tick, 1, columns_tick, 1),
+        (1, 1): lambda: run(streams[0].tick, 2, columns_tick, 2),
+        (2, 1): lambda: streams[1].tick(2),
+        (3, 1): lambda: streams[0].tick(3),
+        (4, 1): lambda: streams[1].tick(3),
+    }
+
+    def tick(k, place):
+        for (step, where), call in ticks.items():
+            if where == place:
+                pl.when(k == step)(call)
 
     def step(k, carry):
         here = pl.ds(pl.multiple_of(k * B, B), B)
-        upper, inverse = factor_tile(whole[k, :, :, here].reshape(B, B))
+        upper, inverse = factor_tile(
+            whole[k, :, :, here].reshape(B, B), lambda: tick(k, 0)
+        )
         upper_o[k] = upper
         dot = functools.partial(
             lax.dot_general, precision=HIGHEST, preferred_element_type=F32
@@ -315,20 +368,18 @@
                             whole[i + 1 :, :, :, : i * B] - update[:, :, :, : i * B]
                         )
                     whole[i + 1 :, :, :, at] = -update[:, :, :, i * B :]
-                if i == 0:
-                    columns_tick(2)
-                if i == 1:
-                    row_ring.tick(2)
-                if i == 3:
-                    row_ring.tick(3)
-                if i == 5:
-                    row_ring.tick(4)
-
+
+        tick(k, 1)
         return carry
 
     lax.fori_loop(0, STEPS, step, 0)
     columns_tick(3)
-    row_ring.finish()
+    for stream in streams:
+        stream.tick(4)
+        stream.finish()
+    to_sibling.wait_send()
+    for d in range(1, 16):
+        block(d, p).wait_send()
     for d in range(1, 16):
         diag(d, p).wait_send()
         piece(d, p).wait_send()
@@ -360,12 +411,15 @@
             pltpu.VMEM((16, 8, B), F32),
             pltpu.VMEM((STEPS, 8, B), F32),
             pltpu.VMEM((8, STEPS, 8, B), F32),
+            pltpu.VMEM((22, 8, B), F32),
+            pltpu.VMEM((16, 22, 8, B), F32),
             pltpu.VMEM((STEPS, 16, 8, W), F32),
             pltpu.VMEM((16, B, B), F32),
             pltpu.VMEM((W, B), F32),
             dma((16,)), dma((16,)), dma((16,)), dma((16,)), dma((8,)), dma((8,)),
             dma((Ring.COUNT,)), dma((Ring.COUNT,)), dma, dma,
-            dma((Ring.COUNT,)), dma((Ring.COUNT,)), dma((8,)), dma((8,)), dma((18,)),
+            dma((Ring.COUNT,)), dma((Ring.COUNT,)), dma((Ring.COUNT,)), dma((Ring.COUNT,)),
+            dma((8,)), dma((8,)), dma((18,)),
         ],
         compiler_params=pltpu.CompilerParams(
             collective_id=0, has_side_effects=True, vmem_limit_bytes=56 * 2**20
@@ -385,112 +439,148 @@
 
 
 PAIR = 2 * B
+PAIRS = 8
+DEPTH = 5
 
 
 def update_kernel(
-    info, c0, c1, c2, c3, c4, c5, upper, inverse, rows_ref, a_ref, o_ref,
-    inverse_h, inverse_l, left_h, left_l, right_h, right_l,
+    step, cout, upper_any, inverse_any, rout, working, out,
+    upper, inverse, columns, rows, mine, inverse_h, inverse_l, left_h, left_l, weight_h, weight_l,
+    fixed_sem, rows_sem, in_sem, out_sem,
 ):
-    m = pl.program_id(0)
-    k0, p, q = info[0], lax.axis_index("row"), lax.axis_index("col")
-
-    @pl.when(m == 0)
-    def _():
-        inverse_h[...], inverse_l[...] = split(inverse[...])
-        parts = [split(c_ref[0]) for c_ref in (c0, c1, c2, c3, c4, c5)]
-        for b in range(0, STEPS, 2):
-            end = (b + 2) * B
-            at = slice(b * B, end)
-            known = [jnp.concatenate([part[i] for part in parts[: b + 2]], 1) for i in range(2)]
-            x = dot3(known, (inverse_h[at, :end], inverse_l[at, :end]), NT)
-            left_h[:, at], left_l[:, at] = split(x)
-
-    first = 2 * m * 8 + q
-    second = first + 8
+    k0, p, q = step[0], lax.axis_index("row"), lax.axis_index("col")
     last = k0 + STEPS - 1
 
-    @pl.when(second > last)
-    def _():
-        x = split(jnp.concatenate([rows_ref[0], rows_ref[1]], 1))
-        for b in range(0, STEPS, 2):
-            end = (b + 2) * B
-            at = slice(b * B, end)
-            y = dot3((inverse_h[at, :end], inverse_l[at, :end]), (x[0][:end], x[1][:end]), NN)
-            right_h[at, :], right_l[at, :] = split(y)
-
-    for part in range(4):
-
-        @pl.when(m // 2 == part)
+    fixed = [
+        pltpu.make_async_copy(inverse_any, inverse, fixed_sem.at[0]),
+        pltpu.make_async_copy(upper_any, upper, fixed_sem.at[1]),
+    ] + [
+        pltpu.make_async_copy(cout.at[lax.rem(k0 + b, 8)], columns.at[b], fixed_sem.at[2 + b])
+        for b in range(STEPS)
+    ]
+
+    def rows_in(m):
+        return pltpu.make_async_copy(rout.at[pl.ds(2 * m, 2)], rows.at[m], rows_sem.at[m])
+
+    def updated(m):
+        return 2 * m * 8 + q + 8 > last
+
+    def start(m):
+        pl.when(updated(m))(rows_in(m).start)
+        mine_in(m).start()
+
+    def mine_in(m):
+        here = pl.ds(pl.multiple_of(m * PAIR, PAIR), PAIR)
+        return pltpu.make_async_copy(working.at[:, here], mine.at[m], in_sem.at[m])
+
+    def mine_out(m):
+        here = pl.ds(pl.multiple_of(m * PAIR, PAIR), PAIR)
+        return pltpu.make_async_copy(mine.at[m], out.at[:, here], out_sem.at[m])
+
+    for copy in fixed:
+        copy.start()
+    fixed[0].wait()
+    for m in range(DEPTH):
+        start(m)
+    inverse_h[...], inverse_l[...] = split(inverse[...])
+    for copy in fixed[1:]:
+        copy.wait()
+    for b in range(0, STEPS, 2):
+        end = (b + 2) * B
+        at = slice(b * B, end)
+        known = split(jnp.concatenate([columns[a] for a in range(b + 2)], 1))
+        x = dot3(known, (inverse_h[at, :end], inverse_l[at, :end]), NT)
+        left_h[:, at], left_l[:, at] = split(x)
+    for b in range(0, STEPS, 2):
+        at = slice(b * B, (b + 2) * B)
+        x = dot3(
+            (left_h[:, b * B :], left_l[:, b * B :]),
+            (inverse_h[b * B :, at], inverse_l[b * B :, at]),
+            NN,
+        )
+        weight_h[:, at], weight_l[:, at] = split(x)
+
+    def pair(m, carry):
+        pl.when(updated(m))(rows_in(m).wait)
+        mine_in(m).wait()
+
+        @pl.when(m + DEPTH < PAIRS)
         def _():
-            top = part * PAIR
-            if part:
-                o_ref[:top, :] = a_ref[:top, :]
-
-            @pl.when(second > last)
+            start(m + DEPTH)
+
+        first = 2 * m * 8 + q
+
+        @pl.when(updated(m))
+        def _():
+            x = split(jnp.concatenate([rows[m, 0], rows[m, 1]], 1))
+            for part in range(4):
+
+                @pl.when(m // 2 == part)
+                def _():
+                    top = part * PAIR
+                    update = dot3((weight_h[top:, :], weight_l[top:, :]), x, NN)
+                    for t in range(top // B, 8):
+                        at = slice(t * B, (t + 1) * B)
+                        for side in range(2):
+                            lanes = slice(side * B, (side + 1) * B)
+                            col = first + 8 * side
+                            keep = (16 * t + p >= col) & (col > last)
+                            part_update = update[t * B - top : (t + 1) * B - top, lanes]
+                            mine[m, at, lanes] = mine[m, at, lanes] - jnp.where(
+                                keep, part_update, 0.0
+                            )
+
+        for side in range(2):
+            col = first + 8 * side
+            lanes = slice(side * B, (side + 1) * B)
+
+            @pl.when((col >= k0) & (col <= last))
             def _():
-                count = 1024 - top
-                update = dot3(
-                    (left_h[top:, :], left_l[top:, :]), (right_h[...], right_l[...]), NN
-                )
-                row = (lax.broadcasted_iota(jnp.int32, (count, PAIR), 0) + top) // B * 16 + p
-                col = lax.broadcasted_iota(jnp.int32, (count, PAIR), 1) // B * 8 + first
-                keep = (row >= col) & (col > last)
-                o_ref[top:, :] = a_ref[top:, :] - jnp.where(keep, update, 0.0)
-
-            @pl.when(second <= last)
-            def _():
-                o_ref[top:, :] = a_ref[top:, :]
-
-    for side in range(2):
-        col = first + 8 * side
-        lanes = slice(side * B, (side + 1) * B)
-        for b in range(STEPS):
-
-            @pl.when(col == k0 + b)
-            def _():
-                solved = left_h[:, b * B : (b + 1) * B].astype(F32) + left_l[
-                    :, b * B : (b + 1) * B
-                ].astype(F32)
+                b = col - k0
+                at = pl.ds(pl.multiple_of(b * B, B), B)
+                solved = left_h[:, at].astype(F32) + left_l[:, at].astype(F32)
                 row = lax.broadcasted_iota(jnp.int32, (1024, B), 0) // B * 16 + p
                 factor = jnp.concatenate([jnp.transpose(upper[b])] * 8, 0)
-                o_ref[:, lanes] = jnp.where(
-                    row > col, solved, jnp.where(row == col, factor, a_ref[:, lanes])
+                mine[m, :, lanes] = jnp.where(
+                    row > col, solved, jnp.where(row == col, factor, mine[m, :, lanes])
                 )
 
+        mine_out(m).start()
+        return carry
+
+    lax.fori_loop(0, PAIRS, pair, 0)
+    for m in range(PAIRS):
+        mine_out(m).wait()
+
 
 def update_call(step, upper, inverse, rout, cout, working):
-    def column(b):
-        return pl.BlockSpec((1, 1024, B), lambda m, info: (lax.rem(info[0] + b, 8), 0, 0))
-
-    def fixed(shape):
-        return pl.BlockSpec(shape, lambda m, info: (0,) * len(shape))
-
+    anywhere = pl.BlockSpec(memory_space=pl.ANY)
+    dma = pltpu.SemaphoreType.DMA
     return pl.pallas_call(
         update_kernel,
         out_shape=jax.ShapeDtypeStruct(working.shape, F32),
-        grid_spec=pltpu.PrefetchScalarGridSpec(
-            num_scalar_prefetch=1,
-            grid=(8,),
-            in_specs=[column(b) for b in range(STEPS)]
-            + [
-                fixed((STEPS, B, B)),
-                fixed((W, W)),
-                pl.BlockSpec((2, W, B), lambda m, info: (m, 0, 0)),
-                pl.BlockSpec((1024, PAIR), lambda m, info: (0, m)),
-            ],
-            out_specs=pl.BlockSpec((1024, PAIR), lambda m, info: (0, m)),
-            scratch_shapes=[
-                pltpu.VMEM((W, W), BF16),
-                pltpu.VMEM((W, W), BF16),
-                pltpu.VMEM((1024, W), BF16),
-                pltpu.VMEM((1024, W), BF16),
-                pltpu.VMEM((W, PAIR), BF16),
-                pltpu.VMEM((W, PAIR), BF16),
-            ],
-        ),
+        in_specs=[pl.BlockSpec(memory_space=pltpu.SMEM)] + [anywhere] * 5,
+        out_specs=anywhere,
+        scratch_shapes=[
+            pltpu.VMEM((STEPS, B, B), F32),
+            pltpu.VMEM((W, W), F32),
+            pltpu.VMEM((STEPS, 1024, B), F32),
+            pltpu.VMEM((PAIRS, 2, W, B), F32),
+            pltpu.VMEM((PAIRS, 1024, PAIR), F32),
+            pltpu.VMEM((W, W), BF16),
+            pltpu.VMEM((W, W), BF16),
+            pltpu.VMEM((1024, W), BF16),
+            pltpu.VMEM((1024, W), BF16),
+            pltpu.VMEM((1024, W), BF16),
+            pltpu.VMEM((1024, W), BF16),
+            dma((8,)),
+            dma((PAIRS,)),
+            dma((PAIRS,)),
+            dma((PAIRS,)),
+        ],
         compiler_params=pltpu.CompilerParams(vmem_limit_bytes=56 * 2**20),
         name="update",
-    )(step, *([cout] * STEPS), upper, inverse, rout, working)
+    )(step, cout, upper, inverse, rout, working)
 
 
 def local(working, step):

time: 108 us -> 95.2 us (0.88)
  Pallas kernels: 106 us -> 93.4 us
    pallas_call x1, Pallas kernels: 88.6 us -> 77.3 us  [gather_call(): pl.pallas_call(gather_kernel, out_shape=(jax.ShapeDtypeStruct((STEPS, B,...]
    pallas_call x1, Pallas kernels: 17.4 us -> 16 us  [update_call(): pl.pallas_call(update_kernel, out_shape=jax.ShapeDtypeStruct(working.shap...]
where the time goes in v3:
time: 95.2 us; the launch traced here: 94.2 us
  Pallas kernels  93.4 us (98%)
    pallas_call x1, Pallas kernels, gather_call(): pl.pallas_call(gather_kernel, out_shape=(jax.ShapeDtypeStruct((STEPS, B,...  77.3 us
    pallas_call x1, Pallas kernels, update_call(): pl.pallas_call(update_kernel, out_shape=jax.ShapeDtypeStruct(working.shap...  16 us

profile of v3, /device:TPU:0, one launch (start us, length us, event | category | flops | bytes accessed | tf_op | source)
XLA Modules:
  0.0 94.2 jit_solution(225247784264065236)
XLA Ops:
  0.7 77.3 %gather_factor.1 = (f32[6,128,128]{2,1,0:T(8,128)}, f32[768,768]{1,0:T(8,128)}, f32[16,768,128]{2,1,0:T(8,128)}, f32[8,1024,128]{2,1,0:T(8,128)}) custom-call(s32[1]{0:T(128)S(6)} %copy.3.step_ref.step, f32[8,128,2048]{2,1,0:T(8,128)} %bitcast.1), custom_call_target="tpu_custom_call" | custom-call | tf_op jit(solution)/shard_map/gather_factor/pallas_call | solution.py:396
  78.0 16.0 %update.1 = f32[1024,2048]{1,0:T(8,128)} custom-call(s32[1]{0:T(128)S(6)} %copy.3.step_ref.step, f32[8,1024,128]{2,1,0:T(8,128)} %get-tuple-element.9.cout, f32[6,128,128]{2,1,0:T(8,128)} %get-tuple-element.10.upper_any, f32[768,768]{1,0:T(8,128)} %get-tuple-element.11.inverse_any, f32[16,768,128]{2,1,0:T(8,128)} %get-tuple-element.12.rout, f32[1024,2048]{1,0:T(8,128)} %working.1), custom_call_target="tpu_custom_call" | custom-call | tf_op jit(solution)/shard_map/update/pallas_call | solution.py:559

commit v4 on v3

--- a/solution.py
+++ b/solution.py
@@ -485,20 +485,26 @@
     inverse_h[...], inverse_l[...] = split(inverse[...])
     for copy in fixed[1:]:
         copy.wait()
-    for b in range(0, STEPS, 2):
-        end = (b + 2) * B
-        at = slice(b * B, end)
-        known = split(jnp.concatenate([columns[a] for a in range(b + 2)], 1))
-        x = dot3(known, (inverse_h[at, :end], inverse_l[at, :end]), NT)
-        left_h[:, at], left_l[:, at] = split(x)
-    for b in range(0, STEPS, 2):
-        at = slice(b * B, (b + 2) * B)
-        x = dot3(
-            (left_h[:, b * B :], left_l[:, b * B :]),
-            (inverse_h[b * B :, at], inverse_l[b * B :, at]),
-            NN,
-        )
-        weight_h[:, at], weight_l[:, at] = split(x)
+    def panel(here):
+        for b in range(0, STEPS, 2):
+            end = (b + 2) * B
+            at = slice(b * B, end)
+            known = split(jnp.concatenate([columns[a, here] for a in range(b + 2)], 1))
+            x = dot3(known, (inverse_h[at, :end], inverse_l[at, :end]), NT)
+            left_h[here, at], left_l[here, at] = split(x)
+        for b in range(0, STEPS, 2):
+            at = slice(b * B, (b + 2) * B)
+            x = dot3(
+                (left_h[here, b * B :], left_l[here, b * B :]),
+                (inverse_h[b * B :, at], inverse_l[b * B :, at]),
+                NN,
+            )
+            weight_h[here, at], weight_l[here, at] = split(x)
+
+    for n in range(2):
+        size = 1024 // 2
+        bottom = (n + 1) * size // B - 1
+        pl.when(16 * bottom + p > k0)(functools.partial(panel, slice(n * size, (n + 1) * size)))
 
     def pair(m, carry):
         pl.when(updated(m))(rows_in(m).wait)

time: 95.2 us -> 94.6 us (level)
  the two profiles are of different devices: /device:TPU:0 before, /device:TPU:2 now
where the time goes in v4:
time: 94.6 us; the launch traced here: 93 us
  Pallas kernels  92.1 us (97%)
    pallas_call x1, Pallas kernels, gather_call(): pl.pallas_call(gather_kernel, out_shape=(jax.ShapeDtypeStruct((STEPS, B,...  76.6 us
    pallas_call x1, Pallas kernels, update_call(): pl.pallas_call(update_kernel, out_shape=jax.ShapeDtypeStruct(working.shap...  15.5 us

profile of v4, /device:TPU:2, one launch (start us, length us, event | category | flops | bytes accessed | tf_op | source)
XLA Modules:
  0.0 93.0 jit_solution(16322599459693638255)
XLA Ops:
  0.7 76.6 %gather_factor.1 = (f32[6,128,128]{2,1,0:T(8,128)}, f32[768,768]{1,0:T(8,128)}, f32[16,768,128]{2,1,0:T(8,128)}, f32[8,1024,128]{2,1,0:T(8,128)}) custom-call(s32[1]{0:T(128)S(6)} %copy.3.step_ref.step, f32[8,128,2048]{2,1,0:T(8,128)} %bitcast.1), custom_call_target="tpu_custom_call" | custom-call | tf_op jit(solution)/shard_map/gather_factor/pallas_call | solution.py:396
  77.3 15.5 %update.1 = f32[1024,2048]{1,0:T(8,128)} custom-call(s32[1]{0:T(128)S(6)} %copy.3.step_ref.step, f32[8,1024,128]{2,1,0:T(8,128)} %get-tuple-element.9.cout, f32[6,128,128]{2,1,0:T(8,128)} %get-tuple-element.10.upper_any, f32[768,768]{1,0:T(8,128)} %get-tuple-element.11.inverse_any, f32[16,768,128]{2,1,0:T(8,128)} %get-tuple-element.12.rout, f32[1024,2048]{1,0:T(8,128)} %working.1), custom_call_target="tpu_custom_call" | custom-call | tf_op jit(solution)/shard_map/update/pallas_call | solution.py:565
